TPU v7x, 768 devices: a whole 4x8x12 slice. The times are simulated.
768 devices in a mesh: segment: 48 (over x, z), ctx: 8 (over y), head: 2 (over core).
Axes of the slice: x: 4, y: 8, z: 12, core: 2. Of those that a mesh axis runs over, the one named last changes fastest.
Arguments:
- inputs: bfloat16 [48, 1024, 5120], P('segment', 'ctx'), may hold values from -6 to 6
- query: bfloat16 [48, 1024, 20, 128], P('segment', 'ctx', 'head'), may hold values from -32 to 32
- grad_out: bfloat16 [48, 1024, 20, 128], P('segment', 'ctx', 'head'), may hold values from -6 to 6
- w_key: bfloat16 [48, 5120, 512], P('segment', None, 'head'), may hold values from -0.078125 to 0.078125
- w_value: bfloat16 [48, 5120, 512], P('segment', None, 'head'), may hold values from -0.078125 to 0.078125
- keep_mask: int32 [1024], replicated, may hold values from 0 to 1
Outputs:
- grad_input: float32 [48, 1024, 5120], P('segment', 'ctx', 'head')
All inputs are finite; a program needn't handle non-finite values.
Results may differ from a plain program's by a relative error of at most 0.022.
The roundings to bfloat16 on the way count: a program that leaves them out, or rounds other values in their place, can miss the bound.
Values may be sent and summed in bfloat16 or wider, within the bound.
A program may use at most 192 MiB of HBM per device.

v0:
```python
import math

import jax
import jax.numpy as jnp
from jax import lax
from jax.sharding import PartitionSpec as P


def prefix(shard, axis, combine, identity):
    length, index = (lax.axis_size(axis), lax.axis_index(axis))
    everything = lax.all_gather(shard.astype(jnp.bfloat16), axis)
    start = jnp.broadcast_to(jnp.asarray(identity, shard.dtype), shard.shape)

    def hop(k, before):
        at = length - 1 - k
        reached = at > index
        new = combine(before, everything[at].astype(shard.dtype))
        return jnp.where(reached, new, before)

    return lax.fori_loop(0, length, hop, start)


def add_terms(earlier, later):
    return earlier + later


def per_device(inputs, query, grad_out, w_key, w_value, keep_mask):
    tok_rows = inputs.shape[1]
    local_heads = query.shape[2]
    head_dim = query.shape[3]
    kv_cols = w_key.shape[2]
    kv_local = kv_cols // head_dim
    group_size = local_heads // kv_local
    scaling = 1.0 / math.sqrt(head_dim)
    tokens = inputs[0]
    key_rows = jnp.dot(tokens, w_key[0], preferred_element_type=jnp.float32).astype(jnp.bfloat16)
    value_rows = jnp.dot(tokens, w_value[0], preferred_element_type=jnp.float32).astype(
        jnp.bfloat16
    )
    keys_all, values_all = (
        lax.all_gather(key_rows, "ctx", axis=0, tiled=True),
        lax.all_gather(value_rows, "ctx", axis=0, tiled=True),
    )
    seq_rows = keys_all.shape[0]
    key_heads = keys_all.reshape(seq_rows, kv_local, head_dim)
    value_heads = values_all.reshape(seq_rows, kv_local, head_dim)
    query_heads = query[0].reshape(tok_rows, kv_local, group_size, head_dim)
    grad_heads = grad_out[0].reshape(tok_rows, kv_local, group_size, head_dim)
    query_major = jnp.moveaxis(query_heads, 1, 0)
    grad_major = jnp.moveaxis(grad_heads, 1, 0)
    ctx_index = lax.axis_index("ctx")
    first_row = ctx_index * tok_rows
    row_pos = first_row + jnp.arange(tok_rows, dtype=jnp.int32)[:, None]
    col_pos = jnp.arange(seq_rows, dtype=jnp.int32)[None, :]
    allowed = (col_pos <= row_pos) & ((keep_mask[None, :] == 1) | (col_pos == row_pos))

    def one_group(packed):
        query_group, grad_group, key_group, value_group = packed
        scores = (
            jnp.einsum("tgd,sd->gts", query_group, key_group, preferred_element_type=jnp.float32)
            * scaling
        )
        masked = jnp.where(allowed, scores, -1e30)
        top_score = jnp.max(masked, axis=-1, keepdims=True)
        totals = jnp.sum(
            jnp.where(allowed, jnp.exp(masked - top_score), 0.0), axis=-1, keepdims=True
        )
        log_total = top_score + jnp.log(totals)
        prob_full = jnp.where(allowed, jnp.exp(masked - log_total), 0.0)
        prob_low = prob_full.astype(jnp.bfloat16)
        attended = jnp.einsum(
            "gts,sd->tgd", prob_low, value_group, preferred_element_type=jnp.float32
        )
        row_dots = jnp.sum(grad_group.astype(jnp.float32) * attended, axis=-1)
        dprob = jnp.einsum(
            "tgd,sd->gts", grad_group, value_group, preferred_element_type=jnp.float32
        )
        score_low = (prob_full * (dprob - jnp.transpose(row_dots, (1, 0))[..., None])).astype(
            jnp.bfloat16
        )
        return (prob_low, score_low)

    probs_b, dscore_b = lax.map(
        one_group,
        (query_major, grad_major, jnp.moveaxis(key_heads, 1, 0), jnp.moveaxis(value_heads, 1, 0)),
    )

    def per_group(packed):
        prob_group, score_group, query_group, grad_group = packed
        value_term = jnp.einsum(
            "gts,tgd->sd", prob_group, grad_group, preferred_element_type=jnp.float32
        )
        key_term = (
            jnp.einsum("gts,tgd->sd", score_group, query_group, preferred_element_type=jnp.float32)
            * scaling
        )
        return (key_term, value_term)

    key_term, value_term = lax.map(per_group, (probs_b, dscore_b, query_major, grad_major))
    key_flat = jnp.moveaxis(key_term, 0, 1).reshape(tok_rows * lax.axis_size("ctx"), kv_cols)
    value_flat = jnp.moveaxis(value_term, 0, 1).reshape(tok_rows * lax.axis_size("ctx"), kv_cols)
    key_grads = lax.psum_scatter(
        jnp.concatenate((key_flat, value_flat), axis=1).astype(jnp.bfloat16),
        "ctx",
        scatter_dimension=0,
        tiled=True,
    ).astype(jnp.float32)
    grad_key = key_grads[:, :kv_cols].astype(jnp.bfloat16)
    grad_value = key_grads[:, kv_cols:].astype(jnp.bfloat16)
    contract = (((1,), (1,)), ((), ()))
    partial_sum = lax.dot_general(grad_key, w_key[0], contract, preferred_element_type=jnp.float32)
    partial_sum = partial_sum + lax.dot_general(
        grad_value, w_value[0], contract, preferred_element_type=jnp.float32
    )
    reduced = lax.psum_scatter(
        partial_sum.astype(jnp.bfloat16), "head", scatter_dimension=1, tiled=True
    ).astype(jnp.float32)
    later = prefix(reduced, "segment", add_terms, jnp.zeros_like(reduced))
    result = reduced + later
    return result[None]


def solution(mesh):
    return jax.shard_map(
        per_device,
        mesh=mesh,
        in_specs=(
            P("segment", "ctx", None),
            P("segment", "ctx", "head", None),
            P("segment", "ctx", "head", None),
            P("segment", None, "head"),
            P("segment", None, "head"),
            P(),
        ),
        out_specs=P("segment", "ctx", "head"),
        check_vma=False,
    )
```

profile of v0, /device:TPU:1, one launch (start us, length us, event | category | flops | bytes accessed | tf_op | source)
XLA Modules:
  0.0 571.0 jit_solution(12255976039623002738)
XLA Ops:
  7.4 3.0 fusion.68
  10.9 22.7 %all_gather.12 = bf16[1024,256]{1,0:T(8,128)(2,1)S(1)} all-gather(bf16[128,256]{1,0:T(8,128)(2,1)S(1)} %fusion.63), channel_id=1, replica_groups=mesh['segment'=48,'ctx'=8,'head'=2] {'ctx'}, dimensions={0}, use_global_device_ids=true | all-gather | bytes 589824 | tf_op jit(solution)/shard_map/all_gather | solution.py:41
  33.6 19.1 %all_gather.13 = bf16[1024,256]{1,0:T(8,128)(2,1)S(1)} all-gather(bf16[128,256]{1,0:T(8,128)(2,1)S(1)} %fusion.68), channel_id=1, replica_groups=mesh['segment'=48,'ctx'=8,'head'=2] {'ctx'}, dimensions={0}, use_global_device_ids=true | all-gather | bytes 589824 | tf_op jit(solution)/shard_map/all_gather | solution.py:42
  53.5 14.2 %while.42 = (s32[]{:T(128)}, bf16[2,5,128,1024]{2,3,1,0:T(8,128)(2,1)}, bf16[2,5,128,1024]{2,3,1,0:T(8,128)(2,1)}, bf16[2,1024,128]{2,1,0:T(8,128)(2,1)S(1)}, bf...) while((s32[]{:T(128)}, ...), condition=%wide.region_4.5_spmd.clone, body=%wide.region_0.4_spmd.clone.sunk | while | flops 515226368 | bytes 63183640 | solution.py:83
  67.7 10.6 %while.41 = (s32[]{:T(128)}, bf16[2,1024,128]{1,2,0:T(8,128)(2,1)}, bf16[2,1024,128]{1,2,0:T(8,128)(2,1)}, bf16[2,5,128,1024]{2,3,1,0:T(8,128)(2,1)}, bf16[2,128...) while((s32[]{:T(128)}, bf16[2,1024,128]{1,2,0:T(8,128)(2,1)}, ...), condition=%wide.region_6.7_spmd, body=%wide.region_5.6_spmd.sunk | while | flops 335806464 | bytes 4786785 | solution.py:99
  83.0 56.1 %reduce-scatter.7.cloned.1.call-done = bf16[128,512]{1,0:T(8,128)(2,1)} async-done(((bf16[1024,512]{1,0:T(8,128)(2,1)}), bf16[128,512]{1,0:T(8,128)(2,1)}) %reduce-scatter.7.cloned.1.call-update) | async-done | bytes 131088
  143.1 25.6 %reduce-scatter.5.cloned.1.call-done = bf16[128,2560]{1,0:T(8,128)(2,1)} async-done(((bf16[128,5120]{1,0:T(8,128)(2,1)}), bf16[128,2560]{1,0:T(8,128)(2,1)}) %reduce-scatter.5.cloned.1.call-update) | async-done | bytes 655376 | tf_op jit(solution)/shard_map/reduce_scatter | solution.py:115
  168.8 263.4 %all-gather.3.cloned.1.call-done = bf16[6144,2560]{1,0:T(8,128)(2,1)} async-done(((bf16[128,2560]{1,0:T(8,128)(2,1)}), bf16[6144,2560]{1,0:T(8,128)(2,1)}) %all-gather.3.cloned.1.call-update) | async-done | bytes 31457296 | tf_op jit(solution)/shard_map/all_gather | solution.py:11
  432.2 129.8 %while.43 = (s32[]{:T(128)}, f32[128,2560]{1,0:T(8,128)}, s32[]{:T(128)}, bf16[48,128,2560]{2,1,0:T(8,128)(2,1)}, s32[]{:T(128)}, /*index=5*/s32[]{:T(128)}, s32[]{:T(128)}, s32[]{:T(128)}) while((s32[]{:T(128)}, f32[128,2560]{1,0:T(8,128)}, s32[]{:T(128)}, bf16[48,128,2560]{2,1,0:T(8,128)(2,1)}, s32[]{:T(128)}, ...), condition=%wide.region_10.11_spmd.clone, body=%wide.region_9.10_spmd.clone.sunk | while | flops 1310728 | bytes 3276963 | solution.py:20
  434.6 2.7 add_select_fusion.2
  437.3 2.7 add_select_fusion.2
  440.0 2.7 add_select_fusion.2
  442.7 2.7 add_select_fusion.2
  445.4 2.7 add_select_fusion.2
  448.1 2.7 add_select_fusion.2
  450.9 2.7 add_select_fusion.2
  453.6 2.7 add_select_fusion.2
  456.3 2.7 add_select_fusion.2
  459.0 2.7 add_select_fusion.2
  461.7 2.7 add_select_fusion.2
  464.4 2.7 add_select_fusion.2
  467.1 2.7 add_select_fusion.2
  469.8 2.7 add_select_fusion.2
  472.5 2.7 add_select_fusion.2
  475.3 2.7 add_select_fusion.2
  478.0 2.7 add_select_fusion.2
  480.7 2.7 add_select_fusion.2
  483.4 2.7 add_select_fusion.2
  486.1 2.7 add_select_fusion.2
  488.8 2.7 add_select_fusion.2
  491.5 2.7 add_select_fusion.2
  494.2 2.7 add_select_fusion.2
  496.9 2.7 add_select_fusion.2
  499.7 2.7 add_select_fusion.2
  502.4 2.7 add_select_fusion.2
  505.1 2.7 add_select_fusion.2
  507.8 2.7 add_select_fusion.2
  510.5 2.7 add_select_fusion.2
  513.2 2.7 add_select_fusion.2
  515.9 2.7 add_select_fusion.2
  518.6 2.7 add_select_fusion.2
  521.3 2.7 add_select_fusion.2
  524.1 2.7 add_select_fusion.2
  526.8 2.7 add_select_fusion.2
  529.5 2.7 add_select_fusion.2
  534.9 2.7 add_select_fusion.2
  543.0 2.7 add_select_fusion.2
  551.2 2.7 add_select_fusion.2
  (88 shorter events, 62.1 us)
Async XLA Ops:
  6.5 3.8 copy-start
  6.5 132.5 %reduce-scatter.7.cloned.1.call-start = ((), (), s32[]{:S(2)}) async-start(), calls=%async_computation.4 | async-start | bytes 1179648
  6.6 3.8 copy-start.7
  10.9 42.6 %copy-start.6 = (bf16[1,128,10,128]{3,1,2,0:T(8,128)(2,1)S(1)}, bf16[1,128,10,128]{3,1,2,0:T(8,128)(2,1)}, u32[]{:S(2)}) copy-start(bf16[1,128,10,128]{3,1,2,0:T(8,128)(2,1)} %param.13) | copy-start | bytes 983044
  53.7 1.1 copy-start.9
  53.8 1.1 copy-start.10
  54.3 1.8 copy-start.1
  55.8 1.8 copy-start.3
  57.6 1.5 copy-start.2
  59.1 1.5 copy-start.4
  60.9 1.1 copy-start.9
  60.9 1.1 copy-start.10
  61.4 1.8 copy-start.1
  62.9 1.8 copy-start.3
  64.7 1.5 copy-start.2
  66.2 1.5 copy-start.4
  82.9 85.9 %reduce-scatter.5.cloned.1.call-start = ((), (), s32[]{:S(2)}) async-start(), calls=%async_computation.2 | async-start | bytes 1966080 | tf_op jit(solution)/shard_map/reduce_scatter | solution.py:115
  139.0 2.0 copy-start.5
  139.0 2.0 copy-start.11
  143.1 289.1 %all-gather.3.cloned.1.call-start = ((), (), s32[]{:S(2)}) async-start(), calls=%async_computation.3 | async-start | bytes 32112640 | tf_op jit(solution)/shard_map/all_gather | solution.py:11
  432.2 129.8 %copy-start.8 = (bf16[128,2560]{1,0:T(8,128)(2,1)S(1)}, bf16[128,2560]{1,0:T(8,128)(2,1)}, u32[]{:S(2)}) copy-start(bf16[128,2560]{1,0:T(8,128)(2,1)} %reduce-scatter.5.cloned.1.call-done) | copy-start | bytes 1966084
Sparse Core Ops, SparseCore 0:
  83.0 55.9 reduce-scatter.6
  143.2 25.5 reduce-scatter.4
  173.0 259.1 all-gather.2
where the time goes:
time: 573 us; the launch traced here: 571 us
  waiting for transfers between devices  345 us (60%)
  other arithmetic  138 us (24%)
  blocking collectives  41.7 us (7%)
  matrix products  21.4 us (4%)
  between operations  13.2 us (2%)
  local copies, waits for them, and re-layouts  11.4 us (2%)
    all_gather x1, waiting for transfers between devices, prefix(): everything = lax.all_gather(shard.astype(jnp.bfloat16), axis)  263 us
    select_n x48, other arithmetic, hop(): return jnp.where(reached, new, before)  130 us
    unnamed x4, waiting for transfers between devices  56.1 us
    reduce_scatter x1, waiting for transfers between devices, per_device(): lax.psum_scatter(partial_sum.astype(jnp.bfloat16), 'head', scatter_dimens...  25.6 us
    all_gather x1, blocking collectives, per_device(): lax.all_gather(key_rows, 'ctx', axis=0, tiled=True)  22.7 us
    all_gather x1, blocking collectives, per_device(): lax.all_gather(value_rows, 'ctx', axis=0, tiled=True)  19.1 us
  transfers between devices with their start and end apart: 3, of which 3 were waited for; matrix products, arithmetic and copies ran while one was open for 0% of the time, Pallas kernels for 0%

commit v1 on v0

v1 whole, which is shorter than its diff:
```python
import functools
import math

import jax
import jax.numpy as jnp
from jax import lax
from jax.experimental import pallas as pl
from jax.experimental.pallas import tpu as pltpu
from jax.sharding import PartitionSpec as P

MESH = pl.DeviceIdType.MESH
BF16 = jnp.bfloat16
F32 = jnp.float32
NX = 4
LAG = 5
ROW_ROW = (((1,), (1,)), ((), ()))


def fdot(a, b):
    return jnp.dot(a, b, preferred_element_type=F32)


def fdot_t(a, b):
    return lax.dot_general(a, b, ROW_ROW, preferred_element_type=F32)


def kernel_body(nz, nctx, x_ref, q_ref, g_ref, wk_ref, wv_ref, keep_ref, o_ref,
                kv, s_buf, dp_buf, rs_in, rs_out, grads, w_oth,
                d_buf, acc, u_in, r_in, l_in, u_out, r_out, l_out,
                ag_ss, ag_rs, rs_ss, rs_rs, w_ss, w_rs, h_ss, h_rs,
                u_ss, u_rs, r_ss, r_rs, l_ss, l_rs, o_sem):
    seg = lax.axis_index("segment")
    b = lax.axis_index("ctx")
    h = lax.axis_index("head")
    x = seg // nz
    z = seg - x * nz
    tok, width = x_ref.shape
    dim = kv.shape[3]
    rows = q_ref.shape[0] // 2
    heads = rows // tok
    half = w_oth.shape[1]
    scaling = 1.0 / math.sqrt(dim)
    xl = lax.rem(x + NX - 1, NX) * nz + z
    xr = lax.rem(x + 1, NX) * nz + z
    zl = x * nz + lax.rem(z + nz - 1, nz)
    zr = x * nz + lax.rem(z + 1, nz)
    yl = lax.rem(b + nctx - 1, nctx)
    yr = lax.rem(b + 1, nctx)

    barrier = pltpu.get_barrier_semaphore()
    for d in ({"segment": xl}, {"segment": xr}, {"segment": zl}, {"segment": zr},
              {"ctx": yl}, {"ctx": yr}, {"head": 1 - h}):
        pl.semaphore_signal(barrier, inc=1, device_id=d, device_id_type=MESH)
    pl.semaphore_wait(barrier, 7)

    def remote(src, dst, ss, rs, where):
        return pltpu.make_async_remote_copy(src, dst, ss, rs, device_id=where, device_id_type=MESH)

    theirs = pl.ds(pl.multiple_of((1 - h) * half, half), half)
    w_copies = [remote(w.at[theirs], w_oth.at[i], w_ss.at[i], w_rs.at[i], {"head": 1 - h})
                for i, w in enumerate((wk_ref, wv_ref))]
    for c in w_copies:
        c.start()

    step_k = 512

    def project(w_ref, i):
        at = pl.ds(pl.multiple_of(i * step_k, step_k), step_k)
        return fdot(x_ref[:, at], w_ref[at, :])

    def proj_step(i, carry):
        return carry[0] + project(wk_ref, i), carry[1] + project(wv_ref, i)
    zero = jnp.zeros((tok, 2 * dim), F32)
    key_rows, value_rows = lax.fori_loop(0, width // step_k, proj_step, (zero, zero))
    kv[b, 0] = key_rows[:, :dim].astype(BF16)
    kv[b, 1] = key_rows[:, dim:].astype(BF16)
    kv[b, 2] = value_rows[:, :dim].astype(BF16)
    kv[b, 3] = value_rows[:, dim:].astype(BF16)

    def up_copy(i, p):
        blk = lax.rem(b - i + nctx, nctx)
        return remote(kv.at[blk, p], kv.at[blk, p], ag_ss.at[i * 4 + p], ag_rs.at[i * 4 + p], {"ctx": yr})

    def up_got(i, p):
        blk = lax.rem(b - 1 - i + nctx, nctx)
        return remote(kv.at[blk, p], kv.at[blk, p], ag_ss.at[i * 4 + p], ag_rs.at[i * 4 + p], {"ctx": yr})

    def down_copy(i, p):
        blk = lax.rem(b + i, nctx)
        j = 16 + i * 4 + p
        return remote(kv.at[blk, p], kv.at[blk, p], ag_ss.at[j], ag_rs.at[j], {"ctx": yl})

    def down_got(i, p):
        blk = lax.rem(b + 1 + i, nctx)
        j = 16 + i * 4 + p
        return remote(kv.at[blk, p], kv.at[blk, p], ag_ss.at[j], ag_rs.at[j], {"ctx": yl})

    for p in range(4):
        up_copy(0, p).start()
        down_copy(0, p).start()

    def score_block(c, tops):
        key_pos = c * tok + lax.broadcasted_iota(jnp.int32, (tok, tok), 0)
        row_pos = b * tok + lax.broadcasted_iota(jnp.int32, (tok, tok), 1)
        at = pl.ds(pl.multiple_of(c * tok, tok), tok)
        kept = jnp.broadcast_to(keep_ref[at, :], (tok, tok))
        allowed = (key_pos <= row_pos) & ((kept == 1) | (key_pos == row_pos))
        limit = jnp.where(allowed, 3e38, -1e30)
        limit = jnp.concatenate([limit] * heads, axis=1)
        new = []
        for g in range(2):
            mine = pl.ds(g * rows, rows)
            s = fdot_t(kv[c, g], q_ref[mine, :]) * scaling
            s = jnp.minimum(s, limit)
            s_buf[g, at, :] = s
            dp_buf[g, at, :] = fdot_t(kv[c, 2 + g], g_ref[mine, :])
            new.append(jnp.maximum(tops[g], jnp.max(s, axis=0, keepdims=True)))
        return tuple(new)

    low = jnp.full((1, rows), -1e30, F32)
    tops = score_block(b, (low, low))

    def gather_step(i, tops):
        for p in range(4):
            up_got(i, p).wait_recv()

            @pl.when(i < 3)
            def _():
                up_copy(i + 1, p).start()

            @pl.when(i < 3)
            def _():
                down_got(i, p).wait_recv()

            @pl.when(i < 2)
            def _():
                down_copy(i + 1, p).start()
        tops = score_block(lax.rem(b - 1 - i + nctx, nctx), tops)
        return lax.cond(i < 3, lambda t: score_block(lax.rem(b + 1 + i, nctx), t), lambda t: t, tops)
    tops = lax.fori_loop(0, 4, gather_step, tops)

    def exp_step(c, sums):
        at = pl.ds(pl.multiple_of(c * tok, tok), tok)
        new = []
        for g in range(2):
            e = jnp.exp(s_buf[g, at, :] - tops[g])
            s_buf[g, at, :] = e
            new.append(sums[g] + jnp.sum(e, axis=0, keepdims=True))
        return tuple(new)
    none = jnp.zeros((1, rows), F32)
    sums = lax.fori_loop(0, nctx, exp_step, (none, none))
    inv = tuple(1.0 / s for s in sums)

    def dots_step(c, dots):
        at = pl.ds(pl.multiple_of(c * tok, tok), tok)
        new = []
        for g in range(2):
            prob = s_buf[g, at, :] * inv[g]
            s_buf[g, at, :] = prob
            low_prob = prob.astype(BF16).astype(F32)
            new.append(dots[g] + jnp.sum(low_prob * dp_buf[g, at, :], axis=0, keepdims=True))
        return tuple(new)
    dots = lax.fori_loop(0, nctx, dots_step, (none, none))

    def grad_block(c):
        at = pl.ds(pl.multiple_of(c * tok, tok), tok)
        out = [None] * 4
        for g in range(2):
            mine = pl.ds(g * rows, rows)
            prob = s_buf[g, at, :]
            ds = (prob * (dp_buf[g, at, :] - dots[g])).astype(BF16)
            out[g] = fdot(ds, q_ref[mine, :]) * scaling
            out[2 + g] = fdot(prob.astype(BF16), g_ref[mine, :])
        return out

    def rs_copy(j, p, where):
        k = j * 4 + p
        return remote(rs_out.at[k], rs_in.at[k], rs_ss.at[k], rs_rs.at[k], where)

    def rs_step(i, carry):
        part = grad_block(lax.rem(b + nctx - 4 + i, nctx))
        for p in range(4):
            k = i * 4 + p

            @pl.when(i > 0)
            def _():
                rs_copy(i - 1, p, {"ctx": yl}).wait_recv()
                rs_out[k] = (part[p] + rs_in[k - 4].astype(F32)).astype(BF16)

            @pl.when(i == 0)
            def _():
                rs_out[k] = part[p].astype(BF16)
            rs_copy(i, p, {"ctx": yl}).start()

        @pl.when(i < 3)
        def _():
            part = grad_block(lax.rem(b + 3 - i, nctx))
            for p in range(4):
                k = (4 + i) * 4 + p

                @pl.when(i > 0)
                def _():
                    rs_copy(3 + i, p, {"ctx": yr}).wait_recv()
                    rs_out[k] = (part[p] + rs_in[k - 4].astype(F32)).astype(BF16)

                @pl.when(i == 0)
                def _():
                    rs_out[k] = part[p].astype(BF16)
                rs_copy(4 + i, p, {"ctx": yr}).start()
        return carry
    lax.fori_loop(0, 4, rs_step, 0)
    part = grad_block(b)
    for p in range(4):
        rs_copy(6, p, {"ctx": yr}).wait_recv()
        rs_copy(3, p, {"ctx": yl}).wait_recv()
        total = part[p] + rs_in[24 + p].astype(F32) + rs_in[12 + p].astype(F32)
        grads[h, :, p * dim:(p + 1) * dim] = total.astype(BF16)
    h_copy = remote(grads.at[h], grads.at[h], h_ss, h_rs, {"head": 1 - h})
    h_copy.start()
    for c in w_copies:
        c.wait_recv()
    remote(grads.at[1 - h], grads.at[1 - h], h_ss, h_rs, {"head": 1 - h}).wait_recv()

    n, _, cols = d_buf.shape
    has_u = x < NX - 1
    off_r = (nz - 1 - z) * LAG
    off_l = z * LAG
    off_f = jnp.maximum(off_r, off_l)

    def u_copy(k):
        return remote(u_out.at[k], u_in.at[k], u_ss.at[k], u_rs.at[k], {"segment": xl})

    def r_copy(k):
        return remote(r_out.at[k], r_in.at[k], r_ss.at[k], r_rs.at[k], {"segment": zl})

    def l_copy(k):
        return remote(l_out.at[k], l_in.at[k], l_ss.at[k], l_rs.at[k], {"segment": zr})

    def o_copy(k):
        at = pl.ds(pl.multiple_of(k * cols, cols), cols)
        return pltpu.make_async_copy(acc.at[k], o_ref.at[:, at], o_sem.at[k])

    def contribution(k):
        own = pl.ds(pl.multiple_of(h * half + k * cols, cols), cols)
        oth = pl.ds(pl.multiple_of(k * cols, cols), cols)
        return (fdot_t(grads[h, :, :2 * dim], wk_ref[own, :]) + fdot_t(grads[h, :, 2 * dim:], wv_ref[own, :])
                + fdot_t(grads[1 - h, :, :2 * dim], w_oth[0, oth, :])
                + fdot_t(grads[1 - h, :, 2 * dim:], w_oth[1, oth, :]))

    def scan_step(t, carry):
        @pl.when(t < n)
        def _():
            k = t
            d_buf[k] = contribution(k)

            @pl.when(has_u)
            def _():
                u_copy(k).wait_recv()
                d_buf[k] = d_buf[k] + u_in[k].astype(F32)

            acc[k] = d_buf[k]

            @pl.when(x > 0)
            def _():
                u_out[k] = d_buf[k].astype(BF16)
                u_copy(k).start()

        k_r = t - off_r

        @pl.when((k_r >= 0) & (k_r < n))
        def _():
            k = k_r

            @pl.when(z < nz - 1)
            def _():
                r_copy(k).wait_recv()
                acc[k] = acc[k] + r_in[k].astype(F32)

            @pl.when((z > 0) & (z < nz - 1))
            def _():
                r_out[k] = (d_buf[k] + r_in[k].astype(F32)).astype(BF16)
                r_copy(k).start()

            @pl.when(z == nz - 1)
            def _():
                r_out[k] = d_buf[k].astype(BF16)
                r_copy(k).start()

        k_l = t - off_l

        @pl.when((k_l >= 0) & (k_l < n) & has_u)
        def _():
            k = k_l

            @pl.when(z > 0)
            def _():
                l_copy(k).wait_recv()
                acc[k] = acc[k] + l_in[k].astype(F32)

            @pl.when((z > 0) & (z < nz - 1))
            def _():
                l_out[k] = (u_in[k].astype(F32) + l_in[k].astype(F32)).astype(BF16)
                l_copy(k).start()

            @pl.when(z == 0)
            def _():
                l_out[k] = u_in[k]
                l_copy(k).start()

        k_f = t - off_f

        @pl.when((k_f >= 0) & (k_f < n))
        def _():
            o_copy(k_f).start()
        return carry
    lax.fori_loop(0, n + (nz - 1) * LAG, scan_step, 0)

    def drain(k, carry):
        o_copy(k).wait()

        @pl.when(x > 0)
        def _():
            u_copy(k).wait_send()

        @pl.when(z > 0)
        def _():
            r_copy(k).wait_send()

        @pl.when((z < nz - 1) & has_u)
        def _():
            l_copy(k).wait_send()
        return carry
    lax.fori_loop(0, n, drain, 0)
    for c in w_copies:
        c.wait_send()
    h_copy.wait_send()

    def drain_ctx(i, carry):
        for p in range(4):
            up_copy(i, p).wait_send()
            rs_copy(i, p, {"ctx": yl}).wait_send()

            @pl.when(i < 3)
            def _():
                down_copy(i, p).wait_send()
                rs_copy(4 + i, p, {"ctx": yr}).wait_send()
        return carry
    lax.fori_loop(0, 4, drain_ctx, 0)


def per_device(nz, nctx, inputs, query, grad_out, w_key, w_value, keep_mask):
    tok, width = inputs.shape[1:]
    heads, dim = query.shape[2:]
    half = width // 2
    cols = 128
    n = half // cols
    rows = heads * tok // 2
    seq = tok * nctx
    major = lambda a: jnp.moveaxis(a[0], 1, 0).reshape(heads * tok, dim)
    dma = pltpu.SemaphoreType.DMA
    out = pl.pallas_call(
        functools.partial(kernel_body, nz, nctx),
        out_shape=jax.ShapeDtypeStruct((tok, half), F32),
        in_specs=[pl.BlockSpec(memory_space=pltpu.VMEM)] * 6,
        out_specs=pl.BlockSpec(memory_space=pl.ANY),
        scratch_shapes=[
            pltpu.VMEM((nctx, 4, tok, dim), BF16),
            pltpu.VMEM((2, seq, rows), F32),
            pltpu.VMEM((2, seq, rows), F32),
            pltpu.VMEM((28, tok, dim), BF16),
            pltpu.VMEM((28, tok, dim), BF16),
            pltpu.VMEM((2, tok, 4 * dim), BF16),
            pltpu.VMEM((2, half, 2 * dim), BF16),
        ] + [pltpu.VMEM((n, tok, cols), F32)] * 2 + [pltpu.VMEM((n, tok, cols), BF16)] * 6
        + [dma((32,)), dma((32,)), dma((28,)), dma((28,)), dma((2,)), dma((2,)), dma, dma]
        + [dma((n,))] * 7,
        compiler_params=pltpu.CompilerParams(
            collective_id=0, has_side_effects=True, vmem_limit_bytes=56 * 2 ** 20),
        name="attention_backward_scan",
    )(inputs[0], major(query), major(grad_out), w_key[0], w_value[0], keep_mask.reshape(seq, 1))
    return out[None]


def solution(mesh):
    return jax.shard_map(
        functools.partial(per_device, mesh.shape["segment"] // NX, mesh.shape["ctx"]),
        mesh=mesh,
        in_specs=(
            P("segment", "ctx", None),
            P("segment", "ctx", "head", None),
            P("segment", "ctx", "head", None),
            P("segment", None, "head"),
            P("segment", None, "head"),
            P(),
        ),
        out_specs=P("segment", "ctx", "head"),
        check_vma=False,
    )
```

time: 573 us -> 120 us (0.21)
  the two profiles are of different devices: /device:TPU:1 before, /device:TPU:8 now
where the time goes in v1:
time: 120 us
  Pallas kernels  115 us (96%)
  local copies, waits for them, and re-layouts  4.17 us (3%)
    pallas_call x1, Pallas kernels, per_device(): pl.pallas_call(functools.partial(kernel_body, nz, nctx), out_shape=jax.Sh...  115 us
    unnamed x1, local copies, waits for them, and re-layouts  2.47 us

profile of v1, /device:TPU:8, one launch (start us, length us, event | category | flops | bytes accessed | tf_op | source)
XLA Modules:
  0.0 119.5 jit_solution(1766565329217745636)
XLA Ops:
  0.0 1.7 %copy.7.keep_ref = s32[1024,1]{1,0:T(8,128)} copy(s32[1024,1]{0,1:T(1,128)} %bitcast.21) | data formatting | bytes 8192 | tf_op jit(solution)/shard_map/reshape | solution.py:380
  1.7 115.4 %attention_backward_scan.1 = f32[128,2560]{1,0:T(8,128)} custom-call(bf16[128,5120]{1,0:T(8,128)(2,1)} %bitcast.18, bf16[1280,128]{1,0:T(8,128)(2,1)} %bitcast.19, bf16[1280,128]{1,0:T(8,128)(2,1)} %bitcast.20, bf16[5120,256]{1,0:T(8,128)(2,1)} %bitcast.16, bf16[5120,256]{1,0:T(8,128)(2,1)} %bitcast.17, s32[1024,1]{1,0:T(8,128)} %copy.7.keep_ref), custom_call_target="tpu_custom_call" | custom-call | tf_op jit(solution)/shard_map/attention_backward_scan/pallas_call | solution.py:361
  117.1 2.5 %copy.9 = f32[1,128,2560]{2,1,0:T(8,128)} copy(f32[1,128,2560]{2,1,0:T(8,128)} %bitcast.15) | data formatting | bytes 2621440

commit v2 on v1

v2 whole, which is shorter than its diff:
```python
import functools
import math

import jax
import jax.numpy as jnp
from jax import lax
from jax.experimental import pallas as pl
from jax.experimental.pallas import tpu as pltpu
from jax.sharding import PartitionSpec as P

MESH = pl.DeviceIdType.MESH
BF16 = jnp.bfloat16
F32 = jnp.float32
NX = 4
LAG = 5
LAGX = 5
PARTS = 2
COLS = 256
SUBS = 1
VMEM_MIB = 56
ROW_ROW = (((1,), (1,)), ((), ()))


def fdot(a, b):
    return jnp.dot(a, b, preferred_element_type=F32)


def fdot_t(a, b):
    return lax.dot_general(a, b, ROW_ROW, preferred_element_type=F32)


def kernel_body(nz, nctx, x_hbm, q_hbm, g_hbm, wk_hbm, wv_hbm, keep_ref, o_ref,
                q_ref, g_ref, x_ref, wk_ref, wv_ref, kv, e_buf, dp_buf, part, rs_in, rs_out, grads, w_oth,
                d_buf, u_buf, acc, a_in, b_in, r_in, l_in, a_out, b_out, r_out, l_out,
                in_sem, qg_sem, ag_ss, ag_rs, rs_ss, rs_rs, w_ss, w_rs, h_ss, h_rs,
                a_ss, a_rs, b_ss, b_rs, r_ss, r_rs, l_ss, l_rs, o_sem):
    seg = lax.axis_index("segment")
    b = lax.axis_index("ctx")
    h = lax.axis_index("head")
    x = seg // nz
    z = seg - x * nz
    tok, width = x_ref.shape
    dim = kv.shape[3]
    rows = q_ref.shape[0] // 2
    heads = rows // tok
    half = w_oth.shape[1]
    sub = tok // PARTS
    scaling = 1.0 / math.sqrt(dim)
    xl = lax.rem(x + NX - 1, NX) * nz + z
    xr = lax.rem(x + 1, NX) * nz + z
    zl = x * nz + lax.rem(z + nz - 1, nz)
    zr = x * nz + lax.rem(z + 1, nz)
    yl = lax.rem(b + nctx - 1, nctx)
    yr = lax.rem(b + 1, nctx)

    barrier = pltpu.get_barrier_semaphore()
    for d in ({"segment": xl}, {"segment": xr}, {"segment": zl}, {"segment": zr},
              {"ctx": yl}, {"ctx": yr}, {"head": 1 - h}):
        pl.semaphore_signal(barrier, inc=1, device_id=d, device_id_type=MESH)

    def remote(src, dst, ss, rs, where):
        return pltpu.make_async_remote_copy(src, dst, ss, rs, device_id=where, device_id_type=MESH)

    steps = in_sem.shape[0] // 3
    step_k = width // steps

    def loads(i):
        at = pl.ds(pl.multiple_of(i * step_k, step_k), step_k)
        return (pltpu.make_async_copy(x_hbm.at[:, at], x_ref.at[:, at], in_sem.at[3 * i]),
                pltpu.make_async_copy(wk_hbm.at[at], wk_ref.at[at], in_sem.at[3 * i + 1]),
                pltpu.make_async_copy(wv_hbm.at[at], wv_ref.at[at], in_sem.at[3 * i + 2]))
    for i in range(steps):
        for c in loads(i):
            c.start()
    qg_loads = [pltpu.make_async_copy(src, dst, qg_sem.at[i])
                for i, (src, dst) in enumerate(((q_hbm, q_ref), (g_hbm, g_ref)))]
    for c in qg_loads:
        c.start()

    def proj_step(i, carry):
        at = pl.ds(pl.multiple_of(i * step_k, step_k), step_k)
        for c in loads(i):
            c.wait()
        xs = x_ref[:, at]
        return carry[0] + fdot(xs, wk_ref[at, :]), carry[1] + fdot(xs, wv_ref[at, :])
    zero = jnp.zeros((tok, 2 * dim), F32)
    key_rows, value_rows = lax.fori_loop(0, steps, proj_step, (zero, zero))
    kv[b, 0] = key_rows[:, :dim].astype(BF16)
    kv[b, 1] = key_rows[:, dim:].astype(BF16)
    kv[b, 2] = value_rows[:, :dim].astype(BF16)
    kv[b, 3] = value_rows[:, dim:].astype(BF16)
    pl.semaphore_wait(barrier, 7)

    def up_copy(i, p):
        blk = lax.rem(b - i + nctx, nctx)
        return remote(kv.at[blk, p], kv.at[blk, p], ag_ss.at[i * 4 + p], ag_rs.at[i * 4 + p], {"ctx": yr})

    def up_got(i, p):
        blk = lax.rem(b - 1 - i + nctx, nctx)
        return remote(kv.at[blk, p], kv.at[blk, p], ag_ss.at[i * 4 + p], ag_rs.at[i * 4 + p], {"ctx": yr})

    def down_copy(i, p):
        blk = lax.rem(b + i, nctx)
        j = 16 + i * 4 + p
        return remote(kv.at[blk, p], kv.at[blk, p], ag_ss.at[j], ag_rs.at[j], {"ctx": yl})

    def down_got(i, p):
        blk = lax.rem(b + 1 + i, nctx)
        j = 16 + i * 4 + p
        return remote(kv.at[blk, p], kv.at[blk, p], ag_ss.at[j], ag_rs.at[j], {"ctx": yl})

    for p in range(4):
        up_copy(0, p).start()
        down_copy(0, p).start()

    theirs = pl.ds(pl.multiple_of((1 - h) * half, half), half)
    w_copies = [remote(w.at[theirs], w_oth.at[i], w_ss.at[i], w_rs.at[i], {"head": 1 - h})
                for i, w in enumerate((wk_ref, wv_ref))]
    for c in w_copies:
        c.start()

    def score_block(c, tops):
        key_pos = c * tok + lax.broadcasted_iota(jnp.int32, (tok, tok), 0)
        row_pos = b * tok + lax.broadcasted_iota(jnp.int32, (tok, tok), 1)
        this = lax.broadcasted_iota(jnp.int32, (nctx, tok), 0) == c
        kept = jnp.sum(jnp.where(this, keep_ref[...].astype(F32), 0.0), axis=0, keepdims=True)
        kept = jnp.broadcast_to(kept, (tok, tok)).T
        allowed = (key_pos <= row_pos) & ((kept == 1.0) | (key_pos == row_pos))
        limit = jnp.where(allowed, 3e38, -1e30)
        limit = jnp.concatenate([limit] * heads, axis=1)
        new = []
        for g in range(2):
            mine = pl.ds(g * rows, rows)
            s = fdot_t(kv[c, g], q_ref[mine, :]) * scaling
            s = jnp.minimum(s, limit)
            dp = fdot_t(kv[c, 2 + g], g_ref[mine, :])
            for p in range(PARTS):
                e_buf[g, p, c] = s[p * sub:(p + 1) * sub]
                dp_buf[g, p, c] = dp[p * sub:(p + 1) * sub]
            new.append(jnp.maximum(tops[g], jnp.max(s, axis=0, keepdims=True)))
        return tuple(new)

    for c in qg_loads:
        c.wait()
    low = jnp.full((1, rows), -1e30, F32)
    tops = score_block(b, (low, low))

    def gather_step(i, tops):
        for p in range(4):
            up_got(i, p).wait_recv()

            @pl.when(i < 3)
            def _():
                up_copy(i + 1, p).start()

            @pl.when(i < 3)
            def _():
                down_got(i, p).wait_recv()

            @pl.when(i < 2)
            def _():
                down_copy(i + 1, p).start()
        tops = score_block(lax.rem(b - 1 - i + nctx, nctx), tops)
        return lax.cond(i < 3, lambda t: score_block(lax.rem(b + 1 + i, nctx), t), lambda t: t, tops)
    tops = lax.fori_loop(0, 4, gather_step, tops)

    def exp_step(c, sums):
        new = []
        for g in range(2):
            total = sums[g]
            for p in range(PARTS):
                e = jnp.exp(e_buf[g, p, c] - tops[g])
                e_buf[g, p, c] = e
                total = total + jnp.sum(e, axis=0, keepdims=True)
            new.append(total)
        return tuple(new)
    none = jnp.zeros((1, rows), F32)
    sums = lax.fori_loop(0, nctx, exp_step, (none, none))
    inv = tuple(1.0 / s for s in sums)

    def dots_step(c, dots):
        new = []
        for g in range(2):
            total = dots[g]
            for p in range(PARTS):
                prob = e_buf[g, p, c] * inv[g]
                e_buf[g, p, c] = prob
                low_prob = prob.astype(BF16).astype(F32)
                total = total + jnp.sum(low_prob * dp_buf[g, p, c], axis=0, keepdims=True)
            new.append(total)
        return tuple(new)
    dots = lax.fori_loop(0, nctx, dots_step, (none, none))

    def make_part(p, q):
        for g in range(2):
            mine = pl.ds(g * rows, rows)
            prob = e_buf[g, p].reshape(nctx * sub, rows)
            if q == 0:
                out = fdot(prob.astype(BF16), g_ref[mine, :])
            else:
                dp = dp_buf[g, p].reshape(nctx * sub, rows)
                out = fdot((prob * (dp - dots[g])).astype(BF16), q_ref[mine, :]) * scaling
            part[p, q, :, :, g * dim:(g + 1) * dim] = out.reshape(nctx, sub, dim)

    def rs_copy(j, p, q):
        k = (j * PARTS + p) * 2 + q
        return remote(rs_out.at[k], rs_in.at[k], rs_ss.at[k], rs_rs.at[k], {"ctx": yl if j < 4 else yr})

    def rs_event(p, q, i):
        for j, blk in ((i, b + nctx - 4 + i), (4 + i, b + 3 - i)):
            if i == 3 and j == 7:
                continue
            k = (j * PARTS + p) * 2 + q
            val = part[p, q, lax.rem(blk, nctx)]
            if i > 0:
                rs_copy(j - 1, p, q).wait_recv()
                val = val + rs_in[k - 2 * PARTS].astype(F32)
            rs_out[k] = val.astype(BF16)
            rs_copy(j, p, q).start()

    def h_copy(p, who):
        at = pl.ds(p * sub, sub)
        return remote(grads.at[who, at], grads.at[who, at], h_ss.at[p], h_rs.at[p], {"head": 1 - h})

    def rs_final(p):
        for q in range(2):
            rs_copy(3, p, q).wait_recv()
            rs_copy(6, p, q).wait_recv()
            total = (part[p, q, b] + rs_in[(3 * PARTS + p) * 2 + q].astype(F32)
                     + rs_in[(6 * PARTS + p) * 2 + q].astype(F32))
            grads[h, p * sub:(p + 1) * sub, q * 2 * dim:(q + 1) * 2 * dim] = total.astype(BF16)
        h_copy(p, h).start()
        h_copy(p, 1 - h).wait_recv()

    for p in range(PARTS):
        for q in range(2):
            make_part(p, q)
            rs_event(p, q, 0)
    for i in range(1, 4):
        for p in range(PARTS):
            for q in range(2):
                rs_event(p, q, i)

    pieces, _, piece = d_buf.shape
    n = pieces // SUBS
    cols = piece * SUBS
    per = n // PARTS
    has_u = x < NX - 1
    off_u = jnp.where(x == NX - 1, 0, jnp.where(x == NX - 2, LAGX, 2 * LAGX))
    off_b = jnp.where(x == NX - 1, LAGX, off_u)
    off_r = off_u + (nz - 1 - z) * LAG
    off_l = off_u + z * LAG
    off_f = jnp.maximum(off_r, off_l)

    def a_copy(k):
        return remote(a_out.at[k], a_in.at[k], a_ss.at[k], a_rs.at[k], {"segment": xl})

    def b_copy(k):
        return remote(b_out.at[k], b_in.at[k], b_ss.at[k], b_rs.at[k], {"segment": xr})

    def r_copy(k):
        return remote(r_out.at[k], r_in.at[k], r_ss.at[k], r_rs.at[k], {"segment": zl})

    def l_copy(k):
        return remote(l_out.at[k], l_in.at[k], l_ss.at[k], l_rs.at[k], {"segment": zr})

    def o_copy(k):
        r = k // (per * SUBS)
        col = (k - r * per * SUBS) * piece
        return pltpu.make_async_copy(
            acc.at[k],
            o_ref.at[pl.ds(pl.multiple_of(r * sub, sub), sub), pl.ds(pl.multiple_of(col, piece), piece)],
            o_sem.at[k])

    def contribution(k):
        r = k // per
        col = (k - r * per) * cols
        own = pl.ds(pl.multiple_of(h * half + col, cols), cols)
        oth = pl.ds(pl.multiple_of(col, cols), cols)
        at = pl.ds(pl.multiple_of(r * sub, sub), sub)
        return (fdot_t(grads[h, at, :2 * dim], wv_ref[own, :]) + fdot_t(grads[h, at, 2 * dim:], wk_ref[own, :])
                + fdot_t(grads[1 - h, at, :2 * dim], w_oth[1, oth, :])
                + fdot_t(grads[1 - h, at, 2 * dim:], w_oth[0, oth, :]))

    def scan_step(t, carry):
        def turn(off, also=True):
            return (t >= off) & (t - off < n) & also

        def parts_of(off):
            return [(t - off) * SUBS + i for i in range(SUBS)]

        @pl.when(t < n)
        def _():
            c = contribution(t)
            for i, k in enumerate(parts_of(0)):
                d_buf[k] = c[:, i * piece:(i + 1) * piece]

            @pl.when((x == 3) | (x == 1))
            def _():
                for k in parts_of(0):
                    a_out[k] = d_buf[k].astype(BF16)
                    a_copy(k).start()

            @pl.when(x == 2)
            def _():
                for k in parts_of(0):
                    b_out[k] = d_buf[k].astype(BF16)
                    b_copy(k).start()

        @pl.when(turn(off_b, x == 3))
        def _():
            for k in parts_of(off_b):
                b_copy(k).wait_recv()
                b_out[k] = (d_buf[k] + b_in[k].astype(F32)).astype(BF16)
                b_copy(k).start()

        @pl.when(turn(off_u, x == 2))
        def _():
            for k in parts_of(off_u):
                a_copy(k).wait_recv()
                u_buf[k] = a_in[k].astype(F32)
                total = d_buf[k] + a_in[k].astype(F32)
                a_out[k] = total.astype(BF16)
                a_copy(k).start()
                d_buf[k] = total

        @pl.when(turn(off_u, x == 1))
        def _():
            for k in parts_of(off_u):
                a_copy(k).wait_recv()
                u_buf[k] = a_in[k].astype(F32)
                d_buf[k] = d_buf[k] + a_in[k].astype(F32)

        @pl.when(turn(off_u, x == 0))
        def _():
            for k in parts_of(off_u):
                a_copy(k).wait_recv()
                b_copy(k).wait_recv()
                u = a_in[k].astype(F32) + b_in[k].astype(F32)
                u_buf[k] = u
                d_buf[k] = d_buf[k] + u

        @pl.when(turn(off_r, z == nz - 1))
        def _():
            for k in parts_of(off_r):
                r_out[k] = d_buf[k].astype(BF16)
                r_copy(k).start()

        @pl.when(turn(off_r, (z > 0) & (z < nz - 1)))
        def _():
            for k in parts_of(off_r):
                r_copy(k).wait_recv()
                total = d_buf[k] + r_in[k].astype(F32)
                r_out[k] = total.astype(BF16)
                r_copy(k).start()

        @pl.when(turn(off_r, z == 0))
        def _():
            for k in parts_of(off_r):
                r_copy(k).wait_recv()

        @pl.when(turn(off_l, has_u & (z == 0)))
        def _():
            for k in parts_of(off_l):
                l_out[k] = u_buf[k].astype(BF16)
                l_copy(k).start()

        @pl.when(turn(off_l, has_u & (z > 0) & (z < nz - 1)))
        def _():
            for k in parts_of(off_l):
                l_copy(k).wait_recv()
                l_out[k] = (u_buf[k] + l_in[k].astype(F32)).astype(BF16)
                l_copy(k).start()

        @pl.when(turn(off_l, has_u & (z == nz - 1)))
        def _():
            for k in parts_of(off_l):
                l_copy(k).wait_recv()

        @pl.when(turn(off_f))
        def _():
            for k in parts_of(off_f):
                acc[k] = d_buf[k]

                @pl.when(z < nz - 1)
                def _():
                    acc[k] = acc[k] + r_in[k].astype(F32)

                @pl.when((z > 0) & has_u)
                def _():
                    acc[k] = acc[k] + l_in[k].astype(F32)
                o_copy(k).start()
        return carry

    rs_final(0)
    for c in w_copies:
        c.wait_recv()
    for p in range(PARTS - 1):
        lax.fori_loop(p * per, (p + 1) * per, scan_step, 0)
        rs_final(p + 1)
    lax.fori_loop((PARTS - 1) * per, n + 2 * LAGX + (nz - 1) * LAG, scan_step, 0)

    def drain(k, carry):
        o_copy(k).wait()

        @pl.when(x > 0)
        def _():
            a_copy(k).wait_send()

        @pl.when(x > 1)
        def _():
            b_copy(k).wait_send()

        @pl.when(z > 0)
        def _():
            r_copy(k).wait_send()

        @pl.when((z < nz - 1) & has_u)
        def _():
            l_copy(k).wait_send()
        return carry
    lax.fori_loop(0, pieces, drain, 0)
    for c in w_copies:
        c.wait_send()
    for p in range(PARTS):
        h_copy(p, h).wait_send()
        for q in range(2):
            for j in range(7):
                rs_copy(j, p, q).wait_send()

    def drain_ctx(i, carry):
        for p in range(4):
            up_copy(i, p).wait_send()

            @pl.when(i < 3)
            def _():
                down_copy(i, p).wait_send()
        return carry
    lax.fori_loop(0, 4, drain_ctx, 0)


def per_device(nz, nctx, inputs, query, grad_out, w_key, w_value, keep_mask):
    tok, width = inputs.shape[1:]
    heads, dim = query.shape[2:]
    half = width // 2
    cols = COLS
    n = half // cols * PARTS
    sub = tok // PARTS
    rows = heads * tok // 2
    kv_cols = w_key.shape[2]
    major = lambda a: jnp.moveaxis(a[0], 1, 0).reshape(heads * tok, dim)
    dma = pltpu.SemaphoreType.DMA
    vmem = pl.BlockSpec(memory_space=pltpu.VMEM)
    hbm = pl.BlockSpec(memory_space=pltpu.HBM)
    nrs = 7 * PARTS * 2
    out = pl.pallas_call(
        functools.partial(kernel_body, nz, nctx),
        out_shape=jax.ShapeDtypeStruct((tok, half), F32),
        in_specs=[hbm, hbm, hbm, hbm, hbm, vmem],
        out_specs=pl.BlockSpec(memory_space=pl.ANY),
        scratch_shapes=[
            pltpu.VMEM((heads * tok, dim), BF16),
            pltpu.VMEM((heads * tok, dim), BF16),
            pltpu.VMEM((tok, width), BF16),
            pltpu.VMEM((width, kv_cols), BF16),
            pltpu.VMEM((width, kv_cols), BF16),
            pltpu.VMEM((nctx, 4, tok, dim), BF16),
            pltpu.VMEM((2, PARTS, nctx, sub, rows), F32),
            pltpu.VMEM((2, PARTS, nctx, sub, rows), F32),
            pltpu.VMEM((PARTS, 2, nctx, sub, 2 * dim), F32),
            pltpu.VMEM((nrs, sub, 2 * dim), BF16),
            pltpu.VMEM((nrs, sub, 2 * dim), BF16),
            pltpu.VMEM((2, tok, 4 * dim), BF16),
            pltpu.VMEM((2, half, 2 * dim), BF16),
        ] + [pltpu.VMEM((n * SUBS, sub, cols // SUBS), F32)] * 3 + [pltpu.VMEM((n * SUBS, sub, cols // SUBS), BF16)] * 8
        + [dma((15,)), dma((2,)), dma((32,)), dma((32,)), dma((nrs,)), dma((nrs,)), dma((2,)), dma((2,)), dma((PARTS,)), dma((PARTS,))]
        + [dma((n * SUBS,))] * 9,
        compiler_params=pltpu.CompilerParams(
            collective_id=0, has_side_effects=True, vmem_limit_bytes=VMEM_MIB * 2 ** 20),
        name="attention_backward_scan",
    )(inputs[0], major(query), major(grad_out), w_key[0], w_value[0], keep_mask.reshape(nctx, tok))
    return out[None]


def solution(mesh):
    return jax.shard_map(
        functools.partial(per_device, mesh.shape["segment"] // NX, mesh.shape["ctx"]),
        mesh=mesh,
        in_specs=(
            P("segment", "ctx", None),
            P("segment", "ctx", "head", None),
            P("segment", "ctx", "head", None),
            P("segment", None, "head"),
            P("segment", None, "head"),
            P(),
        ),
        out_specs=P("segment", "ctx", "head"),
        check_vma=False,
    )
```

time: 120 us -> 112 us (0.933)
  the two profiles are of different devices: /device:TPU:8 before, /device:TPU:16 now
where the time goes in v2:
time: 112 us
  Pallas kernels  109 us (97%)
  local copies, waits for them, and re-layouts  2.47 us (2%)
    pallas_call x1, Pallas kernels, per_device(): pl.pallas_call(functools.partial(kernel_body, nz, nctx), out_shape=jax.Sh...  109 us
    unnamed x1, local copies, waits for them, and re-layouts  2.47 us

profile of v2, /device:TPU:16, one launch (start us, length us, event | category | flops | bytes accessed | tf_op | source)
XLA Modules:
  0.0 111.8 jit_solution(11812342169848351664)
XLA Ops:
  0.0 109.3 %attention_backward_scan.1 = f32[128,2560]{1,0:T(8,128)} custom-call(bf16[128,5120]{1,0:T(8,128)(2,1)} %bitcast.18, bf16[1280,128]{1,0:T(8,128)(2,1)} %bitcast.19, bf16[1280,128]{1,0:T(8,128)(2,1)} %bitcast.20, bf16[5120,256]{1,0:T(8,128)(2,1)} %bitcast.16, bf16[5120,256]{1,0:T(8,128)(2,1)} %bitcast.17, s32[8,128]{1,0:T(8,128)} %bitcast.21), custom_call_target="tpu_custom_call" | custom-call | tf_op jit(solution)/shard_map/attention_backward_scan/pallas_call | solution.py:456
  109.4 2.5 %copy.8 = f32[1,128,2560]{2,1,0:T(8,128)} copy(f32[1,128,2560]{2,1,0:T(8,128)} %bitcast.15) | data formatting | bytes 2621440

commit v3 on v2

--- a/solution.py
+++ b/solution.py
@@ -18,6 +18,8 @@
 COLS = 256
 SUBS = 1
 VMEM_MIB = 56
+HELD = 3
+PIECES = 4
 ROW_ROW = (((1,), (1,)), ((), ()))
 
 
@@ -64,52 +66,53 @@
     steps = in_sem.shape[0] // 3
     step_k = width // steps
 
-    def loads(i):
+    def load(i, j):
         at = pl.ds(pl.multiple_of(i * step_k, step_k), step_k)
-        return (pltpu.make_async_copy(x_hbm.at[:, at], x_ref.at[:, at], in_sem.at[3 * i]),
-                pltpu.make_async_copy(wk_hbm.at[at], wk_ref.at[at], in_sem.at[3 * i + 1]),
-                pltpu.make_async_copy(wv_hbm.at[at], wv_ref.at[at], in_sem.at[3 * i + 2]))
+        src, dst = ((x_hbm.at[:, at], x_ref.at[:, at]), (wk_hbm.at[at], wk_ref.at[at]), (wv_hbm.at[at], wv_ref.at[at]))[j]
+        return pltpu.make_async_copy(src, dst, in_sem.at[3 * i + j])
     for i in range(steps):
-        for c in loads(i):
-            c.start()
+        load(i, 0).start()
+        load(i, 1).start()
+    for i in range(steps):
+        load(i, 2).start()
     qg_loads = [pltpu.make_async_copy(src, dst, qg_sem.at[i])
                 for i, (src, dst) in enumerate(((q_hbm, q_ref), (g_hbm, g_ref)))]
     for c in qg_loads:
         c.start()
 
-    def proj_step(i, carry):
-        at = pl.ds(pl.multiple_of(i * step_k, step_k), step_k)
-        for c in loads(i):
-            c.wait()
-        xs = x_ref[:, at]
-        return carry[0] + fdot(xs, wk_ref[at, :]), carry[1] + fdot(xs, wv_ref[at, :])
-    zero = jnp.zeros((tok, 2 * dim), F32)
-    key_rows, value_rows = lax.fori_loop(0, steps, proj_step, (zero, zero))
-    kv[b, 0] = key_rows[:, :dim].astype(BF16)
-    kv[b, 1] = key_rows[:, dim:].astype(BF16)
-    kv[b, 2] = value_rows[:, :dim].astype(BF16)
-    kv[b, 3] = value_rows[:, dim:].astype(BF16)
+    def project(w_ref, waits, at_kv):
+        def proj_step(i, total):
+            at = pl.ds(pl.multiple_of(i * step_k, step_k), step_k)
+            for j in waits:
+                load(i, j).wait()
+            return total + fdot(x_ref[:, at], w_ref[at, :])
+        out = lax.fori_loop(0, steps, proj_step, jnp.zeros((tok, 2 * dim), F32))
+        kv[b, at_kv] = out[:, :dim].astype(BF16)
+        kv[b, at_kv + 1] = out[:, dim:].astype(BF16)
+
+    def ctx_copy(blk, p, j, where):
+        at = pl.ds(p * (4 // PIECES), 4 // PIECES)
+        return remote(kv.at[blk, at], kv.at[blk, at], ag_ss.at[j + p], ag_rs.at[j + p], where)
+
+    def up_copy(i, p):
+        return ctx_copy(lax.rem(b - i + nctx, nctx), p, i * PIECES, {"ctx": yr})
+
+    def up_got(i, p):
+        return ctx_copy(lax.rem(b - 1 - i + nctx, nctx), p, i * PIECES, {"ctx": yr})
+
+    def down_copy(i, p):
+        return ctx_copy(lax.rem(b + i, nctx), p, (4 + i) * PIECES, {"ctx": yl})
+
+    def down_got(i, p):
+        return ctx_copy(lax.rem(b + 1 + i, nctx), p, (4 + i) * PIECES, {"ctx": yl})
+
+    project(wk_ref, (0, 1), 0)
     pl.semaphore_wait(barrier, 7)
-
-    def up_copy(i, p):
-        blk = lax.rem(b - i + nctx, nctx)
-        return remote(kv.at[blk, p], kv.at[blk, p], ag_ss.at[i * 4 + p], ag_rs.at[i * 4 + p], {"ctx": yr})
-
-    def up_got(i, p):
-        blk = lax.rem(b - 1 - i + nctx, nctx)
-        return remote(kv.at[blk, p], kv.at[blk, p], ag_ss.at[i * 4 + p], ag_rs.at[i * 4 + p], {"ctx": yr})
-
-    def down_copy(i, p):
-        blk = lax.rem(b + i, nctx)
-        j = 16 + i * 4 + p
-        return remote(kv.at[blk, p], kv.at[blk, p], ag_ss.at[j], ag_rs.at[j], {"ctx": yl})
-
-    def down_got(i, p):
-        blk = lax.rem(b + 1 + i, nctx)
-        j = 16 + i * 4 + p
-        return remote(kv.at[blk, p], kv.at[blk, p], ag_ss.at[j], ag_rs.at[j], {"ctx": yl})
-
-    for p in range(4):
+    for p in range(PIECES // 2):
+        up_copy(0, p).start()
+        down_copy(0, p).start()
+    project(wv_ref, (2,), 2)
+    for p in range(PIECES // 2, PIECES):
         up_copy(0, p).start()
         down_copy(0, p).start()
 
@@ -146,7 +149,7 @@
     tops = score_block(b, (low, low))
 
     def gather_step(i, tops):
-        for p in range(4):
+        for p in range(PIECES):
             up_got(i, p).wait_recv()
 
             @pl.when(i < 3)
@@ -282,7 +285,50 @@
                 + fdot_t(grads[1 - h, at, :2 * dim], w_oth[1, oth, :])
                 + fdot_t(grads[1 - h, at, 2 * dim:], w_oth[0, oth, :]))
 
+    ends = (z == 0) | (z == nz - 1)
+
+    def drain_sends():
+        def drain(k, carry):
+            @pl.when(x > 0)
+            def _():
+                a_copy(k).wait_send()
+
+            @pl.when(x > 1)
+            def _():
+                b_copy(k).wait_send()
+
+            @pl.when(z > 0)
+            def _():
+                r_copy(k).wait_send()
+
+            @pl.when((z < nz - 1) & has_u)
+            def _():
+                l_copy(k).wait_send()
+            return carry
+        lax.fori_loop(0, pieces, drain, 0)
+        for c in w_copies:
+            c.wait_send()
+        for p in range(PARTS):
+            h_copy(p, h).wait_send()
+            for q in range(2):
+                for j in range(7):
+                    rs_copy(j, p, q).wait_send()
+
+        def drain_ctx(i, carry):
+            for p in range(PIECES):
+                up_copy(i, p).wait_send()
+
+                @pl.when(i < 3)
+                def _():
+                    down_copy(i, p).wait_send()
+            return carry
+        lax.fori_loop(0, 4, drain_ctx, 0)
+
     def scan_step(t, carry):
+        @pl.when(ends & (t == off_f - 2))
+        def _():
+            drain_sends()
+
         def turn(off, also=True):
             return (t >= off) & (t - off < n) & also
 
@@ -390,6 +436,10 @@
                 def _():
                     acc[k] = acc[k] + l_in[k].astype(F32)
                 o_copy(k).start()
+
+                @pl.when(k >= HELD)
+                def _():
+                    o_copy(k - HELD).wait()
         return carry
 
     rs_final(0)
@@ -400,43 +450,14 @@
         rs_final(p + 1)
     lax.fori_loop((PARTS - 1) * per, n + 2 * LAGX + (nz - 1) * LAG, scan_step, 0)
 
-    def drain(k, carry):
+    @pl.when(jnp.logical_not(ends))
+    def _():
+        drain_sends()
+
+    def drain_out(k, carry):
         o_copy(k).wait()
-
-        @pl.when(x > 0)
-        def _():
-            a_copy(k).wait_send()
-
-        @pl.when(x > 1)
-        def _():
-            b_copy(k).wait_send()
-
-        @pl.when(z > 0)
-        def _():
-            r_copy(k).wait_send()
-
-        @pl.when((z < nz - 1) & has_u)
-        def _():
-            l_copy(k).wait_send()
         return carry
-    lax.fori_loop(0, pieces, drain, 0)
-    for c in w_copies:
-        c.wait_send()
-    for p in range(PARTS):
-        h_copy(p, h).wait_send()
-        for q in range(2):
-            for j in range(7):
-                rs_copy(j, p, q).wait_send()
-
-    def drain_ctx(i, carry):
-        for p in range(4):
-            up_copy(i, p).wait_send()
-
-            @pl.when(i < 3)
-            def _():
-                down_copy(i, p).wait_send()
-        return carry
-    lax.fori_loop(0, 4, drain_ctx, 0)
+    lax.fori_loop(pieces - HELD, pieces, drain_out, 0)
 
 
 def per_device(nz, nctx, inputs, query, grad_out, w_key, w_value, keep_mask):
@@ -473,7 +494,7 @@
             pltpu.VMEM((2, tok, 4 * dim), BF16),
             pltpu.VMEM((2, half, 2 * dim), BF16),
         ] + [pltpu.VMEM((n * SUBS, sub, cols // SUBS), F32)] * 3 + [pltpu.VMEM((n * SUBS, sub, cols // SUBS), BF16)] * 8
-        + [dma((15,)), dma((2,)), dma((32,)), dma((32,)), dma((nrs,)), dma((nrs,)), dma((2,)), dma((2,)), dma((PARTS,)), dma((PARTS,))]
+        + [dma((15,)), dma((2,)), dma((8 * PIECES,)), dma((8 * PIECES,)), dma((nrs,)), dma((nrs,)), dma((2,)), dma((2,)), dma((PARTS,)), dma((PARTS,))]
         + [dma((n * SUBS,))] * 9,
         compiler_params=pltpu.CompilerParams(
             collective_id=0, has_side_effects=True, vmem_limit_bytes=VMEM_MIB * 2 ** 20),

time: 112 us -> 111 us (level)
  the two profiles are of different devices: /device:TPU:16 before, /device:TPU:8 now
where the time goes in v3:
time: 111 us; the launch traced here: 110 us
  Pallas kernels  108 us (97%)
  local copies, waits for them, and re-layouts  2.47 us (2%)
    pallas_call x1, Pallas kernels, per_device(): pl.pallas_call(functools.partial(kernel_body, nz, nctx), out_shape=jax.Sh...  108 us
    unnamed x1, local copies, waits for them, and re-layouts  2.47 us

profile of v3, /device:TPU:8, one launch (start us, length us, event | category | flops | bytes accessed | tf_op | source)
XLA Modules:
  0.0 110.4 jit_solution(7851795524677947304)
XLA Ops:
  0.0 107.9 %attention_backward_scan.1 = f32[128,2560]{1,0:T(8,128)} custom-call(bf16[128,5120]{1,0:T(8,128)(2,1)} %bitcast.18, bf16[1280,128]{1,0:T(8,128)(2,1)} %bitcast.19, bf16[1280,128]{1,0:T(8,128)(2,1)} %bitcast.20, bf16[5120,256]{1,0:T(8,128)(2,1)} %bitcast.16, bf16[5120,256]{1,0:T(8,128)(2,1)} %bitcast.17, s32[8,128]{1,0:T(8,128)} %bitcast.21), custom_call_target="tpu_custom_call" | custom-call | tf_op jit(solution)/shard_map/attention_backward_scan/pallas_call | solution.py:477
  107.9 2.5 %copy.8 = f32[1,128,2560]{2,1,0:T(8,128)} copy(f32[1,128,2560]{2,1,0:T(8,128)} %bitcast.15) | data formatting | bytes 2621440

commit v4 on v3

--- a/solution.py
+++ b/solution.py
@@ -32,7 +32,7 @@
 
 
 def kernel_body(nz, nctx, x_hbm, q_hbm, g_hbm, wk_hbm, wv_hbm, keep_ref, o_ref,
-                q_ref, g_ref, x_ref, wk_ref, wv_ref, kv, e_buf, dp_buf, part, rs_in, rs_out, grads, w_oth,
+                q_ref, g_ref, x_ref, wk_ref, wv_ref, kv, e_buf, dp_buf, top_buf, sum_buf, part, rs_in, rs_out, grads, w_oth,
                 d_buf, u_buf, acc, a_in, b_in, r_in, l_in, a_out, b_out, r_out, l_out,
                 in_sem, qg_sem, ag_ss, ag_rs, rs_ss, rs_rs, w_ss, w_rs, h_ss, h_rs,
                 a_ss, a_rs, b_ss, b_rs, r_ss, r_rs, l_ss, l_rs, o_sem):
@@ -137,10 +137,14 @@
             s = fdot_t(kv[c, g], q_ref[mine, :]) * scaling
             s = jnp.minimum(s, limit)
             dp = fdot_t(kv[c, 2 + g], g_ref[mine, :])
+            top = jnp.max(s, axis=0, keepdims=True)
+            e = jnp.exp(s - top)
             for p in range(PARTS):
-                e_buf[g, p, c] = s[p * sub:(p + 1) * sub]
+                e_buf[g, p, c] = e[p * sub:(p + 1) * sub]
                 dp_buf[g, p, c] = dp[p * sub:(p + 1) * sub]
-            new.append(jnp.maximum(tops[g], jnp.max(s, axis=0, keepdims=True)))
+            top_buf[c, g] = top
+            sum_buf[c, g] = jnp.sum(e, axis=0, keepdims=True)
+            new.append(jnp.maximum(tops[g], top))
         return tuple(new)
 
     for c in qg_loads:
@@ -167,18 +171,15 @@
         return lax.cond(i < 3, lambda t: score_block(lax.rem(b + 1 + i, nctx), t), lambda t: t, tops)
     tops = lax.fori_loop(0, 4, gather_step, tops)
 
-    def exp_step(c, sums):
+    def weigh_step(c, sums):
         new = []
         for g in range(2):
-            total = sums[g]
-            for p in range(PARTS):
-                e = jnp.exp(e_buf[g, p, c] - tops[g])
-                e_buf[g, p, c] = e
-                total = total + jnp.sum(e, axis=0, keepdims=True)
-            new.append(total)
+            weight = jnp.exp(top_buf[c, g] - tops[g])
+            top_buf[c, g] = weight
+            new.append(sums[g] + weight * sum_buf[c, g])
         return tuple(new)
     none = jnp.zeros((1, rows), F32)
-    sums = lax.fori_loop(0, nctx, exp_step, (none, none))
+    sums = lax.fori_loop(0, nctx, weigh_step, (none, none))
     inv = tuple(1.0 / s for s in sums)
 
     def dots_step(c, dots):
@@ -186,7 +187,7 @@
         for g in range(2):
             total = dots[g]
             for p in range(PARTS):
-                prob = e_buf[g, p, c] * inv[g]
+                prob = e_buf[g, p, c] * (top_buf[c, g] * inv[g])
                 e_buf[g, p, c] = prob
                 low_prob = prob.astype(BF16).astype(F32)
                 total = total + jnp.sum(low_prob * dp_buf[g, p, c], axis=0, keepdims=True)
@@ -488,6 +489,8 @@
             pltpu.VMEM((nctx, 4, tok, dim), BF16),
             pltpu.VMEM((2, PARTS, nctx, sub, rows), F32),
             pltpu.VMEM((2, PARTS, nctx, sub, rows), F32),
+            pltpu.VMEM((nctx, 2, 1, rows), F32),
+            pltpu.VMEM((nctx, 2, 1, rows), F32),
             pltpu.VMEM((PARTS, 2, nctx, sub, 2 * dim), F32),
             pltpu.VMEM((nrs, sub, 2 * dim), BF16),
             pltpu.VMEM((nrs, sub, 2 * dim), BF16),

time: 111 us -> 110 us (level)
  no operation moved by 1% of the time
where the time goes in v4:
time: 110 us
  Pallas kernels  107 us (97%)
  local copies, waits for them, and re-layouts  2.47 us (2%)
    pallas_call x1, Pallas kernels, per_device(): pl.pallas_call(functools.partial(kernel_body, nz, nctx), out_shape=jax.Sh...  107 us
    unnamed x1, local copies, waits for them, and re-layouts  2.47 us

profile of v4, /device:TPU:8, one launch (start us, length us, event | category | flops | bytes accessed | tf_op | source)
XLA Modules:
  0.0 109.7 jit_solution(18370058880722572438)
XLA Ops:
  0.0 107.3 %attention_backward_scan.1 = f32[128,2560]{1,0:T(8,128)} custom-call(bf16[128,5120]{1,0:T(8,128)(2,1)} %bitcast.18, bf16[1280,128]{1,0:T(8,128)(2,1)} %bitcast.19, bf16[1280,128]{1,0:T(8,128)(2,1)} %bitcast.20, bf16[5120,256]{1,0:T(8,128)(2,1)} %bitcast.16, bf16[5120,256]{1,0:T(8,128)(2,1)} %bitcast.17, s32[8,128]{1,0:T(8,128)} %bitcast.21), custom_call_target="tpu_custom_call" | custom-call | tf_op jit(solution)/shard_map/attention_backward_scan/pallas_call | solution.py:478
  107.3 2.5 %copy.8 = f32[1,128,2560]{2,1,0:T(8,128)} copy(f32[1,128,2560]{2,1,0:T(8,128)} %bitcast.15) | data formatting | bytes 2621440
